TPU v7x, 32 devices: a whole 2x2x4 slice. The times are simulated.
32 devices in a mesh: rows: 2 (over x), chan: 16 (over z, y, core).
Axes of the slice: x: 2, y: 2, z: 4, core: 2. Of those that a mesh axis runs over, the one named last changes fastest.
Arguments:
- pair_rep: bfloat16 [512, 512, 128], P('rows', 'chan'), may hold values from -6 to 6
- upstream: bfloat16 [512, 512, 128], P('rows', 'chan'), may hold values from -8 to 8
- out_proj: bfloat16 [128, 512], replicated, may hold values from -0.5 to 0.5
- out_gate: bfloat16 [128, 128], replicated, may hold values from -0.5 to 0.5
- out_final: bfloat16 [128, 128], replicated, may hold values from -0.5 to 0.5
- in_proj: bfloat16 [128, 512], replicated, may hold values from -0.5 to 0.5
- in_gate: bfloat16 [128, 128], replicated, may hold values from -0.5 to 0.5
- in_final: bfloat16 [128, 128], replicated, may hold values from -0.5 to 0.5
- out_drop: int32 [512, 128], P('chan'), may hold values 0 or 1
- in_drop: int32 [512, 128], P('chan'), may hold values 0 or 1
Outputs:
- final_pair: bfloat16 [512, 512, 128], P('rows', 'chan')
- grad_pair: bfloat16 [512, 512, 128], P('rows', 'chan')
- grad_proj: float32 [128, 512], replicated
- grad_gate: float32 [128, 128], replicated
- grad_final: float32 [128, 128], replicated
All inputs are finite; a program needn't handle non-finite values. No bound on the sum of `out_drop` or of `in_drop` on one device may be relied on, other than what follows from the above.
Results may differ from a plain program's by a relative error of at most 0.0097.
Values may be sent and summed in bfloat16 or wider, within the bound.
A program may use at most 192 MiB of HBM per device.

v0:
```python
import jax
import jax.numpy as jnp
from jax import lax
from jax.sharding import PartitionSpec as P

N = 512


epsilon = 1e-05
keep_rate = 0.75


def layer_norm(values, along):
    average = jnp.mean(values, axis=along, keepdims=True)
    centred = values - average
    inv_std = lax.rsqrt(jnp.mean(centred * centred, axis=along, keepdims=True) + epsilon)
    return (centred * inv_std, inv_std)


def norm_back(gradient, scaled, inv_std, along):
    first_mean = jnp.mean(gradient, axis=along, keepdims=True)
    second_mean = jnp.mean(gradient * scaled, axis=along, keepdims=True)
    return inv_std * (gradient - first_mean - scaled * second_mean)


def front(pair_in, proj_w, gate_w):
    row_count, col_count, channels = pair_in.shape
    scaled, inv_std = layer_norm(pair_in.astype(jnp.float32), 2)
    normed = scaled.astype(jnp.bfloat16).reshape(-1, channels)
    projected = lax.dot_general(
        proj_w, normed, (((0,), (1,)), ((), ())), preferred_element_type=jnp.float32
    )
    hidden = projected.shape[0] // 4
    gate_act = jax.nn.sigmoid(jnp.dot(normed, gate_w, preferred_element_type=jnp.float32))
    left_proj = (jax.nn.sigmoid(projected[:hidden]) * projected[hidden : 2 * hidden]).astype(
        jnp.bfloat16
    )
    right_proj = (
        jax.nn.sigmoid(projected[2 * hidden : 3 * hidden]) * projected[3 * hidden :]
    ).astype(jnp.bfloat16)
    left_proj = left_proj.reshape(hidden, row_count, col_count)
    right_proj = right_proj.reshape(hidden, row_count, col_count)
    return (scaled, inv_std, normed, projected, gate_act, left_proj, right_proj)


def finish(triangle, gate_act, final_w, pair_in, drop_mask):
    hidden = triangle.shape[0]
    tri_hat, tri_inv = layer_norm(triangle.reshape(hidden, -1).astype(jnp.float32), 0)
    tri_normed = tri_hat.astype(jnp.bfloat16)
    out_rows = lax.dot_general(
        tri_normed, final_w, (((0,), (0,)), ((), ())), preferred_element_type=jnp.float32
    )
    update = gate_act * out_rows
    new_pair = (
        pair_in.astype(jnp.float32)
        + drop_mask.astype(jnp.float32)[None] * update.reshape(pair_in.shape) / keep_rate
    ).astype(jnp.bfloat16)
    return (tri_hat, tri_inv, tri_normed, out_rows, new_pair)


def shards(
    pair_rep, upstream, out_proj, out_gate, out_final, in_proj, in_gate, in_final, out_drop, in_drop
):
    channels = pair_rep.shape[2]
    scaled, inv_std, normed, projected, gate_act, left_proj, right_proj = front(
        pair_rep, out_proj, out_gate
    )
    hidden = left_proj.shape[0]
    left_slab, right_slab = (
        lax.all_to_all(left_proj, "chan", split_axis=0, concat_axis=2, tiled=True),
        lax.all_to_all(right_proj, "chan", split_axis=0, concat_axis=2, tiled=True),
    )
    triangle = jnp.einsum(
        "hik,hjk->hij",
        left_slab,
        lax.all_gather(right_slab, "rows", axis=1, tiled=True),
        preferred_element_type=jnp.float32,
    )
    tri_pairs = lax.all_to_all(
        triangle.astype(jnp.bfloat16), "chan", split_axis=2, concat_axis=0, tiled=True
    )
    tri_hat, tri_inv, tri_normed, out_rows, middle = finish(
        tri_pairs, gate_act, out_final, pair_rep, out_drop
    )
    update_grad = (
        upstream.astype(jnp.float32) * out_drop.astype(jnp.float32)[None] / keep_rate
    ).reshape(-1, channels)
    gate_grad = update_grad * out_rows
    out_grad = (update_grad * gate_act).astype(jnp.bfloat16)
    normed_grad = lax.dot_general(
        out_final, out_grad, (((1,), (1,)), ((), ())), preferred_element_type=jnp.float32
    )
    tri_grad = (
        norm_back(normed_grad, tri_hat, tri_inv, 0).astype(jnp.bfloat16).reshape(left_proj.shape)
    )
    pre_grad = (gate_grad * gate_act * (1.0 - gate_act)).astype(jnp.bfloat16)
    tri_slab = lax.all_to_all(tri_grad, "chan", split_axis=0, concat_axis=2, tiled=True)
    right_again = lax.all_gather(right_slab, "rows", axis=1, tiled=True)
    left_grad = jnp.einsum(
        "hij,hjk->hik", tri_slab, right_again, preferred_element_type=jnp.float32
    ).astype(jnp.bfloat16)
    left_full = lax.all_gather(left_slab, "rows", axis=1, tiled=True)
    tri_cols = lax.all_to_all(tri_slab, "rows", split_axis=2, concat_axis=1, tiled=True)
    right_grad = jnp.einsum(
        "hij,hik->hjk", tri_cols, left_full, preferred_element_type=jnp.float32
    ).astype(jnp.bfloat16)
    left_pairs, right_pairs = (
        lax.all_to_all(left_grad, "chan", split_axis=2, concat_axis=0, tiled=True),
        lax.all_to_all(right_grad, "chan", split_axis=2, concat_axis=0, tiled=True),
    )
    left_back = left_pairs.reshape(hidden, -1).astype(jnp.float32)
    right_back = right_pairs.reshape(hidden, -1).astype(jnp.float32)
    left_sig = jax.nn.sigmoid(projected[:hidden])
    right_sig = jax.nn.sigmoid(projected[2 * hidden : 3 * hidden])
    proj_grad = jnp.concatenate(
        [
            left_back * projected[hidden : 2 * hidden] * left_sig * (1.0 - left_sig),
            left_back * left_sig,
            right_back * projected[3 * hidden :] * right_sig * (1.0 - right_sig),
            right_back * right_sig,
        ],
        0,
    ).astype(jnp.bfloat16)
    input_grad = lax.dot_general(
        proj_grad, out_proj, (((0,), (1,)), ((), ())), preferred_element_type=jnp.float32
    )
    input_grad = input_grad + lax.dot_general(
        pre_grad, out_gate, (((1,), (1,)), ((), ())), preferred_element_type=jnp.float32
    )
    grad_pair = (
        upstream.astype(jnp.float32)
        + norm_back(input_grad.reshape(pair_rep.shape), scaled, inv_std, 2)
    ).astype(jnp.bfloat16)
    grad_proj = lax.dot_general(
        normed, proj_grad, (((0,), (1,)), ((), ())), preferred_element_type=jnp.float32
    )
    grad_gate = lax.dot_general(
        normed, pre_grad, (((0,), (0,)), ((), ())), preferred_element_type=jnp.float32
    )
    grad_final = jnp.dot(tri_normed, out_grad, preferred_element_type=jnp.float32)
    summed = lax.psum((grad_proj, grad_gate, grad_final), ("rows", "chan"))
    two_parts = front(middle, in_proj, in_gate)
    gate_two, left_two, right_two = (two_parts[4], two_parts[5], two_parts[6])
    left_chan, right_chan = (
        lax.all_to_all(left_two, "chan", split_axis=0, concat_axis=2, tiled=True),
        lax.all_to_all(right_two, "chan", split_axis=0, concat_axis=2, tiled=True),
    )
    left_cols = lax.all_to_all(left_chan, "rows", split_axis=2, concat_axis=1, tiled=True)
    tri_two = jnp.einsum(
        "hki,hkj->hij",
        left_cols,
        lax.all_gather(right_chan, "rows", axis=1, tiled=True),
        preferred_element_type=jnp.float32,
    )
    tri_two_pairs = lax.all_to_all(
        tri_two.astype(jnp.bfloat16), "chan", split_axis=2, concat_axis=0, tiled=True
    )
    final_pair = finish(tri_two_pairs, gate_two, in_final, middle, in_drop)[4]
    return (final_pair, grad_pair, summed[0] / N, summed[1] / N, summed[2] / N)


def solution(mesh):
    in_specs = (
        P("rows", "chan", None),
        P("rows", "chan", None),
        P(),
        P(),
        P(),
        P(),
        P(),
        P(),
        P("chan", None),
        P("chan", None),
    )
    out_specs = (P("rows", "chan", None), P("rows", "chan", None), P(), P(), P())
    return jax.shard_map(shards, mesh=mesh, in_specs=in_specs, out_specs=out_specs, check_vma=False)
```

profile of v0, /device:TPU:0, one launch (start us, length us, event | category | flops | bytes accessed | tf_op | source)
XLA Modules:
  0.0 948.5 jit_solution(11422155511641581754)
XLA Ops:
  10.2 8.1 fusion.18
  36.9 54.7 %all_to_all.162 = bf16[128,256,32]{1,2,0:T(8,128)(2,1)S(1)} all-to-all(bf16[128,256,32]{1,2,0:T(8,128)(2,1)} %copy.103), channel_id=1, replica_groups=mesh['rows'=2,'chan'=16] {'chan'}, dimensions={0} | all-to-all | bytes 4194304 | tf_op jit(solution)/shard_map/all_to_all | solution.py:71
  101.9 52.4 %all_to_all.163 = bf16[128,256,32]{1,2,0:T(8,128)(2,1)S(1)} all-to-all(bf16[128,256,32]{1,2,0:T(8,128)(2,1)} %copy.101), channel_id=1, replica_groups=mesh['rows'=2,'chan'=16] {'chan'}, dimensions={0} | all-to-all | bytes 4194304 | tf_op jit(solution)/shard_map/all_to_all | solution.py:70
  165.8 5.7 all-to-all-start.2
  175.8 36.8 %all-to-all-done.2 = bf16[8,256,512]{1,0,2:T(8,128)(2,1)} async-done(((bf16[8,256,512]{1,0,2:T(8,128)(2,1)}), bf16[8,256,512]{1,0,2:T(8,128)(2,1)}, u32[]{:S(2)}, u32[]{:S(2)}) %all-to-all-start.2) | async-done | bytes 2097184 | tf_op jit(solution)/shard_map/all_to_all | solution.py:79
  221.2 10.5 %copy.109 = f32[16,8,256,32]{3,2,1,0:T(8,128)} copy(f32[16,8,256,32]{2,3,0,1:T(8,128)} %get-tuple-element.27) | data formatting | bytes 8388608 | tf_op jit(solution)/shard_map/convert_element_type | solution.py:48
  231.7 13.0 %reshape.194 = f32[128,8192]{1,0:T(8,128)} reshape(f32[16,8,256,32]{3,2,1,0:T(8,128)} %copy.109) | data formatting | bytes 8388608 | tf_op jit(solution)/shard_map/convert_element_type | solution.py:48
  250.2 6.1 fusion.45
  273.1 8.1 fusion.39
  286.1 58.5 %all_to_all.164 = bf16[128,256,32]{1,2,0:T(8,128)(2,1)S(1)} all-to-all(bf16[128,256,32]{1,2,0:T(8,128)(2,1)} %copy.128), channel_id=1, replica_groups=mesh['rows'=2,'chan'=16] {'chan'}, dimensions={0} | all-to-all | bytes 4194304 | tf_op jit(solution)/shard_map/all_to_all | solution.py:97
  367.7 21.2 %all-to-all-done.9 = bf16[8,256,512]{1,0,2:T(8,128)(2,1)} async-done(((bf16[8,256,512]{1,0,2:T(8,128)(2,1)}), bf16[8,256,512]{1,0,2:T(8,128)(2,1)}, u32[]{:S(2)}, u32[]{:S(2)}) %all-to-all-start.9) | async-done | bytes 2097184 | tf_op jit(solution)/shard_map/all_to_all | solution.py:103
  402.9 21.8 %all-gather.8.cloned.1.call-done = bf16[8,512,512]{2,1,0:T(8,128)(2,1)} async-done(((bf16[8,256,512]{2,1,0:T(8,128)(2,1)}), bf16[8,512,512]{2,1,0:T(8,128)(2,1)}) %all-gather.8.cloned.1.call-update) | async-done | bytes 4194320 | tf_op jit(solution)/shard_map/all_gather | solution.py:102
  434.6 11.0 %all-to-all-start.10 = ((bf16[8,256,512]{1,0,2:T(8,128)(2,1)}), bf16[8,256,512]{1,0,2:T(8,128)(2,1)}, u32[]{:S(2)}, u32[]{:S(2)}) async-start(bf16[8,256,512]{1,0,2:T(8,128)(2,1)} %copy.139), calls=%async_computation.10 | async-start | bytes 4194304 | tf_op jit(solution)/shard_map/all_to_all | solution.py:109
  450.1 10.5 %copy.133 = f32[16,8,256,32]{3,2,1,0:T(8,128)} copy(f32[16,8,256,32]{2,3,0,1:T(8,128)} %convert_bitcast_fusion.1) | data formatting | bytes 8388608 | tf_op jit(solution)/shard_map/convert_element_type | solution.py:111
  460.6 13.0 %reshape.196 = f32[128,8192]{1,0:T(8,128)} reshape(f32[16,8,256,32]{3,2,1,0:T(8,128)} %copy.133) | data formatting | bytes 8388608 | tf_op jit(solution)/shard_map/convert_element_type | solution.py:111
  473.6 5.6 copy.134
  479.3 7.5 all-to-all-done.10
  491.3 10.5 %copy.141 = f32[16,8,256,32]{3,2,1,0:T(8,128)} copy(f32[16,8,256,32]{2,3,0,1:T(8,128)} %convert_bitcast_fusion) | data formatting | bytes 8388608 | tf_op jit(solution)/shard_map/convert_element_type | solution.py:112
  501.7 13.0 %reshape.197 = f32[128,8192]{1,0:T(8,128)} reshape(f32[16,8,256,32]{3,2,1,0:T(8,128)} %copy.141) | data formatting | bytes 8388608 | tf_op jit(solution)/shard_map/convert_element_type | solution.py:112
  520.3 10.2 %multiply_convert_fusion.3 = (bf16[128,8192]{0,1:T(8,128)(2,1)S(1)}, bf16[128,8192]{0,1:T(8,128)(2,1)S(1)}, bf16[128,8192]{0,1:T(8,128)(2,1)S(1)}, bf16[128,8192]{0,1:T(8,128)(2,1)S(1)}) fusion(f32[128,8192]{0,1:T(8,128)} %copy.134, f32[512,8192]{0,1:T(8,128)} %copy-done.2, f32[128,8192]{0,1:T(8,128)} %copy.142), kind=kLoop, calls=%fused_computation.77 | loop fusion | flops 20971520 | bytes 33554432 | tf_op jit(solution)/shard_map/convert.16
  537.2 10.6 %fusion.15 = f32[256,32]{1,0:T(8,128)S(1)} fusion(f32[256,32,128]{2,1,0:T(8,128)} %bitcast.131, bf16[256,32,128]{2,1,0:T(8,128)(2,1)S(1)} %copy-done.4, f32[256,32]{1,0:T(8,128)S(1)} %add_rsqrt_fusion.3, f32[256,32]{1,0:T(8,128)S(1)} %broadcast_multiply_fusion.5), kind=kLoop, calls=%fused_computation.30 | loop fusion | flops 5234688 | bytes 6389760 | tf_op jit(solution)/shard_map/reduce_sum | solution.py:22
  547.9 8.3 convert_reduce_fusion
  556.3 7.4 fusion.13
  578.5 11.3 %all-to-all-start.5 = ((bf16[128,256,32]{1,2,0:T(8,128)(2,1)}), bf16[128,256,32]{1,2,0:T(8,128)(2,1)}, u32[]{:S(2)}, u32[]{:S(2)}) async-start(bf16[128,256,32]{1,2,0:T(8,128)(2,1)} %copy.119), calls=%async_computation.5 | async-start | bytes 4194304 | tf_op jit(solution)/shard_map/all_to_all | solution.py:146
  593.3 37.6 %all-to-all-done.5 = bf16[128,256,32]{1,2,0:T(8,128)(2,1)} async-done(((bf16[128,256,32]{1,2,0:T(8,128)(2,1)}), bf16[128,256,32]{1,2,0:T(8,128)(2,1)}, u32[]{:S(2)}, u32[]{:S(2)}) %all-to-all-start.5) | async-done | bytes 2097184 | tf_op jit(solution)/shard_map/all_to_all | solution.py:146
  630.9 11.2 %all-to-all-start.3 = ((bf16[128,256,32]{1,2,0:T(8,128)(2,1)}), bf16[128,256,32]{1,2,0:T(8,128)(2,1)S(1)}, u32[]{:S(2)}, u32[]{:S(2)}) async-start(bf16[128,256,32]{1,2,0:T(8,128)(2,1)} %copy.114), calls=%async_computation.3 | async-start | bytes 4194304 | tf_op jit(solution)/shard_map/all_to_all | solution.py:145
  649.3 33.9 %all-to-all-done.3 = bf16[128,256,32]{1,2,0:T(8,128)(2,1)S(1)} async-done(((bf16[128,256,32]{1,2,0:T(8,128)(2,1)}), bf16[128,256,32]{1,2,0:T(8,128)(2,1)S(1)}, u32[]{:S(2)}, u32[]{:S(2)}) %all-to-all-start.3) | async-done | bytes 2097184 | tf_op jit(solution)/shard_map/all_to_all | solution.py:145
  684.6 44.2 %all_to_all.165 = bf16[8,256,512]{1,0,2:T(8,128)(2,1)S(1)} all-to-all(bf16[8,256,512]{1,0,2:T(8,128)(2,1)S(1)} %copy.116), channel_id=1, replica_groups=mesh['rows'=2,'chan'=16] {'rows'}, dimensions={2} | all-to-all | bytes 4194304 | tf_op jit(solution)/shard_map/all_to_all | solution.py:148
  743.8 5.7 all-to-all-start.6
  761.8 139.5 %all-reduce.3.cloned.1.call-done = (f32[128,512]{1,0:T(8,128)}, f32[128,128]{1,0:T(8,128)}, f32[128,128]{1,0:T(8,128)}) async-done(((f32[128,512]{1,0:T(8,128)}, f32[128,128]{1,0:T(8,128)}, f32[128,128]{1,0:T(8,128)}), (f32[128,512]{1,0:T(8,128)}, f32[128,128]{1,0:T(8,128)}, f32[128,128]{1,0:T(8,128)})) %all-reduce.3.cloned.1.call-update) | async-done | bytes 393232 | tf_op jit(solution)/shard_map/psum | solution.py:141
  911.5 10.7 %copy.124 = f32[16,8,256,32]{3,2,1,0:T(8,128)} copy(f32[16,8,256,32]{2,3,0,1:T(8,128)} %get-tuple-element.25) | data formatting | bytes 8388608 | tf_op jit(solution)/shard_map/convert_element_type | solution.py:48
  922.2 13.1 %reshape.195 = f32[128,8192]{1,0:T(8,128)} reshape(f32[16,8,256,32]{3,2,1,0:T(8,128)} %copy.124) | data formatting | bytes 8388608 | tf_op jit(solution)/shard_map/convert_element_type | solution.py:48
  (170 shorter events, 222.2 us)
Async XLA Ops:
  7.2 15.5 %copy-start = (bf16[128,512]{1,0:T(8,128)(2,1)S(1)}, bf16[128,512]{1,0:T(8,128)(2,1)}, u32[]{:S(2)}) copy-start(bf16[128,512]{1,0:T(8,128)(2,1)} %param.12) | copy-start | bytes 393220
  7.2 11.1 %copy-start.4 = (bf16[256,32,128]{2,1,0:T(8,128)(2,1)S(1)}, bf16[256,32,128]{2,1,0:T(8,128)(2,1)}, u32[]{:S(2)}) copy-start(bf16[256,32,128]{2,1,0:T(8,128)(2,1)} %param.10) | copy-start | bytes 6291460
  7.2 148.6 %all-gather.4.cloned.1.call-start = ((), (), s32[]{:S(2)}) async-start(), calls=%async_computation.11 | async-start | bytes 6291456 | tf_op jit(solution)/shard_map/all_gather | solution.py:76
  25.0 7.0 copy-start.2
  161.3 10.2 %copy-start.32 = (s32[32,128]{1,0:T(8,128)S(1)}, s32[32,128]{1,0:T(8,128)}, u32[]{:S(2)}) copy-start(s32[32,128]{1,0:T(8,128)} %param.18) | copy-start | bytes 49156
  165.8 46.8 %all-to-all-start.2 = ((bf16[8,256,512]{1,0,2:T(8,128)(2,1)}), bf16[8,256,512]{1,0,2:T(8,128)(2,1)}, u32[]{:S(2)}, u32[]{:S(2)}) async-start(bf16[8,256,512]{1,0,2:T(8,128)(2,1)} %copy.107), calls=%async_computation.2 | async-start | bytes 4194304 | tf_op jit(solution)/shard_map/all_to_all | solution.py:79
  250.2 7.4 copy-start.29
  260.5 4.4 copy-start.3
  264.8 4.9 copy-start.20
  348.7 40.2 %all-to-all-start.9 = ((bf16[8,256,512]{1,0,2:T(8,128)(2,1)}), bf16[8,256,512]{1,0,2:T(8,128)(2,1)}, u32[]{:S(2)}, u32[]{:S(2)}) async-start(bf16[8,256,512]{1,0,2:T(8,128)(2,1)} %copy.136), calls=%async_computation.9 | async-start | bytes 4194304 | tf_op jit(solution)/shard_map/all_to_all | solution.py:103
  353.5 71.2 %all-gather.8.cloned.1.call-start = ((), (), s32[]{:S(2)}) async-start(), calls=%async_computation.13 | async-start | bytes 6291456 | tf_op jit(solution)/shard_map/all_gather | solution.py:102
  388.9 45.7 %all-to-all-start.8 = ((bf16[8,256,512]{1,0,2:T(8,128)(2,1)}), bf16[8,256,512]{1,0,2:T(8,128)(2,1)}, u32[]{:S(2)}, u32[]{:S(2)}) async-start(bf16[8,256,512]{1,0,2:T(8,128)(2,1)} %copy.131), calls=%async_computation.8 | async-start | bytes 4194304 | tf_op jit(solution)/shard_map/all_to_all | solution.py:108
  434.6 52.1 %all-to-all-start.10 = ((bf16[8,256,512]{1,0,2:T(8,128)(2,1)}), bf16[8,256,512]{1,0,2:T(8,128)(2,1)}, u32[]{:S(2)}, u32[]{:S(2)}) async-start(bf16[8,256,512]{1,0,2:T(8,128)(2,1)} %copy.139), calls=%async_computation.10 | async-start | bytes 4194304 | tf_op jit(solution)/shard_map/all_to_all | solution.py:109
  530.5 3.4 copy-start.27
  530.5 3.4 copy-start.18
  537.2 10.7 %copy-start.5 = (f32[8192,128]{1,0:T(8,128)S(1)}, f32[8192,128]{1,0:T(8,128)}, u32[]{:S(2)}) copy-start(f32[8192,128]{1,0:T(8,128)} %get-tuple-element.32) | copy-start | bytes 12582916
  537.2 10.7 %copy-start.17 = (bf16[256,32,128]{2,1,0:T(8,128)(2,1)S(1)}, bf16[256,32,128]{2,1,0:T(8,128)(2,1)}, u32[]{:S(2)}) copy-start(bf16[256,32,128]{2,1,0:T(8,128)(2,1)} %param.11) | copy-start | bytes 6291460
  556.2 10.5 %copy-start.6 = (bf16[256,32,128]{2,1,0:T(8,128)(2,1)}, bf16[256,32,128]{2,1,0:T(8,128)(2,1)S(1)}, u32[]{:S(2)}) copy-start(bf16[256,32,128]{2,1,0:T(8,128)(2,1)S(1)} %get-tuple-element.9) | copy-start | bytes 6291460
  556.2 11.9 %copy-start.28 = (bf16[128,512]{1,0:T(8,128)(2,1)S(1)}, bf16[128,512]{1,0:T(8,128)(2,1)}, u32[]{:S(2)}) copy-start(bf16[128,512]{1,0:T(8,128)(2,1)} %param.15) | copy-start | bytes 393220
  578.5 52.4 %all-to-all-start.5 = ((bf16[128,256,32]{1,2,0:T(8,128)(2,1)}), bf16[128,256,32]{1,2,0:T(8,128)(2,1)}, u32[]{:S(2)}, u32[]{:S(2)}) async-start(bf16[128,256,32]{1,2,0:T(8,128)(2,1)} %copy.119), calls=%async_computation.5 | async-start | bytes 4194304 | tf_op jit(solution)/shard_map/all_to_all | solution.py:146
  630.9 52.3 %all-to-all-start.3 = ((bf16[128,256,32]{1,2,0:T(8,128)(2,1)}), bf16[128,256,32]{1,2,0:T(8,128)(2,1)S(1)}, u32[]{:S(2)}, u32[]{:S(2)}) async-start(bf16[128,256,32]{1,2,0:T(8,128)(2,1)} %copy.114), calls=%async_computation.3 | async-start | bytes 4194304 | tf_op jit(solution)/shard_map/all_to_all | solution.py:145
  642.1 91.5 %all-gather.6.cloned.1.call-start = ((), (), s32[]{:S(2)}) async-start(), calls=%async_computation.12 | async-start | bytes 6291456 | tf_op jit(solution)/shard_map/all_gather | solution.py:152
  739.1 10.4 %copy-start.33 = (s32[32,128]{1,0:T(8,128)S(1)}, s32[32,128]{1,0:T(8,128)}, u32[]{:S(2)}) copy-start(s32[32,128]{1,0:T(8,128)} %param.19) | copy-start | bytes 49156
  739.1 10.4 %copy-start.9 = (bf16[128,8192]{0,1:T(8,128)(2,1)S(1)}, bf16[128,8192]{0,1:T(8,128)(2,1)}, u32[]{:S(2)}) copy-start(bf16[128,8192]{0,1:T(8,128)(2,1)} %copy-done.8) | copy-start | bytes 6291460
  743.8 162.1 %all-to-all-start.6 = ((bf16[8,256,512]{1,0,2:T(8,128)(2,1)}), bf16[8,256,512]{1,0,2:T(8,128)(2,1)}, u32[]{:S(2)}, u32[]{:S(2)}) async-start(bf16[8,256,512]{1,0,2:T(8,128)(2,1)} %copy.122), calls=%async_computation.6 | async-start | bytes 4194304 | tf_op jit(solution)/shard_map/all_to_all | solution.py:155
  749.4 151.8 %all-reduce.3.cloned.1.call-start = ((), (), s32[]{:S(2)}) async-start(), calls=%async_computation.14 | async-start | bytes 786432 | tf_op jit(solution)/shard_map/psum | solution.py:141
  749.5 4.6 copy-start.23
  749.6 4.5 copy-start.25
  754.1 4.4 copy-start.16
  754.1 4.5 copy-start.34
  922.2 13.1 %copy-start.31 = (bf16[128,128]{1,0:T(8,128)(2,1)S(1)}, bf16[128,128]{1,0:T(8,128)(2,1)}, u32[]{:S(2)}) copy-start(bf16[128,128]{1,0:T(8,128)(2,1)} %param.17) | copy-start | bytes 98308
  935.3 4.4 copy-start.7
  (14 other events, 29.9 us)
Sparse Core Ops, SparseCore 0:
  97.2 57.1 all-gather.3
  357.8 66.8 all-gather.7
  649.4 72.7 all-gather.5
  758.7 142.5 all-reduce.2
where the time goes:
time: 960 us; the launch traced here: 949 us
  waiting for transfers between devices  298 us (31%)
  blocking collectives  210 us (22%)
  local copies, waits for them, and re-layouts  207 us (22%)
  other arithmetic  106 us (11%)
  matrix products  58.3 us (6%)
  starting transfers between devices  54.4 us (6%)
  between operations  14.6 us (2%)
    psum x1, waiting for transfers between devices, shards(): summed = lax.psum((grad_proj, grad_gate, grad_final), ('rows', 'chan'))  139 us
    all_to_all x1, blocking collectives, shards(): lax.all_to_all(tri_grad, 'chan', split_axis=0, concat_axis=2, tiled=True)  58.5 us
    all_to_all x1, blocking collectives, shards(): lax.all_to_all(right_proj, 'chan', split_axis=0, concat_axis=2, tiled=True)  54.7 us
    convert_element_type x5, local copies, waits for them, and re-layouts, finish(): triangle.reshape(hidden, -1).astype(jnp.float32)  52.8 us
    all_to_all x1, blocking collectives, shards(): lax.all_to_all(left_proj, 'chan', split_axis=0, concat_axis=2, tiled=True)  52.4 us
    all_to_all x1, blocking collectives, shards(): lax.all_to_all(left_chan, 'rows', split_axis=2, concat_axis=1, tiled=True)  44.2 us
    all_to_all x1, waiting for transfers between devices, shards(): lax.all_to_all(right_two, 'chan', split_axis=0, concat_axis=2, tiled=True)  37.6 us
    all_to_all x1, waiting for transfers between devices, shards(): lax.all_to_all(triangle.astype(jnp.bfloat16), 'chan', split_axis=2, conca...  36.8 us
  transfers between devices with their start and end apart: 11, of which 7 were waited for; matrix products, arithmetic and copies ran while one was open for 11% of the time, Pallas kernels for 0%

commit v1 on v0

--- a/solution.py
+++ b/solution.py
@@ -1,13 +1,262 @@
+import functools
+
 import jax
 import jax.numpy as jnp
 from jax import lax
+from jax.experimental import pallas as pl
+from jax.experimental.pallas import tpu as pltpu
 from jax.sharding import PartitionSpec as P
 
 N = 512
-
+H = 128
 
 epsilon = 1e-05
 keep_rate = 0.75
+
+BOTH = ("rows", "chan")
+STEP = 4
+GRANT = 40 * 1024 * 1024
+F32 = jnp.float32
+BF16 = jnp.bfloat16
+NN = (((1,), (0,)), ((), ()))
+NT = (((1,), (1,)), ((), ()))
+TN = (((0,), (0,)), ((), ()))
+
+
+def mm(a, b, dims=NN):
+    return lax.dot_general(a, b, dims, preferred_element_type=F32)
+
+
+def norm_cols(x):
+    average = jnp.mean(x, axis=0, keepdims=True)
+    centred = x - average
+    inv_std = lax.rsqrt(jnp.mean(centred * centred, axis=0, keepdims=True) + epsilon)
+    return centred * inv_std, inv_std
+
+
+def sides(normed, proj_t, left_ref, right_ref, at):
+    hidden = proj_t.shape[0] // 4
+    projected = mm(proj_t, normed)
+    a_gate, a_val = projected[:hidden], projected[hidden : 2 * hidden]
+    b_gate, b_val = projected[2 * hidden : 3 * hidden], projected[3 * hidden :]
+    left_ref[at] = (jax.nn.sigmoid(a_gate) * a_val).astype(BF16)
+    right_ref[at] = (jax.nn.sigmoid(b_gate) * b_val).astype(BF16)
+
+
+def front_kernel(pair_ref, proj_ref, left_ref, right_ref):
+    for at in range(pair_ref.shape[0]):
+        scaled, _ = norm_cols(pair_ref[at].astype(F32))
+        sides(scaled.astype(BF16), proj_ref[...], left_ref, right_ref, at)
+
+
+def middle_kernel(
+    tri_ref, pair_ref, up_ref, drop_ref, gate_ref, final_t_ref, final_ref, proj_two_ref,
+    mid_ref, tri_grad_ref, pre_ref, left_ref, right_ref, grad_gate_ref, grad_final_ref,
+):
+    @pl.when(pl.program_id(0) == 0)
+    def _():
+        grad_gate_ref[...] = jnp.zeros_like(grad_gate_ref)
+        grad_final_ref[...] = jnp.zeros_like(grad_final_ref)
+
+    for at in range(tri_ref.shape[0]):
+        pair = pair_ref[at].astype(F32)
+        normed = norm_cols(pair)[0].astype(BF16)
+        gate = jax.nn.sigmoid(mm(gate_ref[...], normed))
+        tri_hat, tri_inv = norm_cols(tri_ref[at].astype(F32))
+        tri_normed = tri_hat.astype(BF16)
+        out_rows = mm(final_t_ref[...], tri_normed)
+        drop = drop_ref[at]
+        middle = (pair + drop * (gate * out_rows)).astype(BF16)
+        mid_ref[at] = middle
+        update_grad = up_ref[at].astype(F32) * drop
+        out_grad = (update_grad * gate).astype(BF16)
+        pre_grad = (update_grad * out_rows * gate * (1.0 - gate)).astype(BF16)
+        pre_ref[at] = pre_grad
+        normed_grad = mm(final_ref[...], out_grad)
+        first = jnp.mean(normed_grad, axis=0, keepdims=True)
+        second = jnp.mean(normed_grad * tri_hat, axis=0, keepdims=True)
+        tri_grad_ref[at] = (tri_inv * (normed_grad - first - tri_hat * second)).astype(BF16)
+        grad_gate_ref[...] += mm(normed, pre_grad, NT)
+        grad_final_ref[...] += mm(tri_normed, out_grad, NT)
+        normed_two = norm_cols(middle.astype(F32))[0].astype(BF16)
+        sides(normed_two, proj_two_ref[...], left_ref, right_ref, at)
+
+
+def back_kernel(
+    pair_ref, up_ref, pre_ref, left_ref, right_ref, proj_t_ref, proj_ref, gate_ref,
+    grad_ref, grad_proj_ref,
+):
+    @pl.when(pl.program_id(0) == 0)
+    def _():
+        grad_proj_ref[...] = jnp.zeros_like(grad_proj_ref)
+
+    hidden = proj_t_ref.shape[0] // 4
+    for at in range(pair_ref.shape[0]):
+        scaled, inv_std = norm_cols(pair_ref[at].astype(F32))
+        normed = scaled.astype(BF16)
+        projected = mm(proj_t_ref[...], normed)
+        left, right = left_ref[at].astype(F32), right_ref[at].astype(F32)
+        left_sig = jax.nn.sigmoid(projected[:hidden])
+        right_sig = jax.nn.sigmoid(projected[2 * hidden : 3 * hidden])
+        left_val, right_val = left * left_sig, right * right_sig
+        proj_grad = jnp.concatenate(
+            [
+                (left_val * projected[hidden : 2 * hidden] * (1.0 - left_sig)).astype(BF16),
+                left_val.astype(BF16),
+                (right_val * projected[3 * hidden :] * (1.0 - right_sig)).astype(BF16),
+                right_val.astype(BF16),
+            ],
+            0,
+        )
+        grad_proj_ref[...] += mm(normed, proj_grad, NT)
+        input_grad = mm(proj_ref[...], proj_grad) + mm(gate_ref[...], pre_ref[at])
+        first = jnp.mean(input_grad, axis=0, keepdims=True)
+        second = jnp.mean(input_grad * scaled, axis=0, keepdims=True)
+        grad_ref[at] = (
+            up_ref[at].astype(F32) + inv_std * (input_grad - first - scaled * second)
+        ).astype(BF16)
+
+
+def final_kernel(tri_ref, mid_ref, drop_ref, gate_ref, final_t_ref, out_ref):
+    for at in range(tri_ref.shape[0]):
+        middle = mid_ref[at].astype(F32)
+        gate = jax.nn.sigmoid(mm(gate_ref[...], norm_cols(middle)[0].astype(BF16)))
+        tri_normed = norm_cols(tri_ref[at].astype(F32))[0].astype(BF16)
+        out_rows = mm(final_t_ref[...], tri_normed)
+        out_ref[at] = (middle + drop_ref[at] * (gate * out_rows)).astype(BF16)
+
+
+def pairwise(kernel, by_pair, whole, pair_outs, sum_outs, name):
+    steps = by_pair[0].shape[0] // STEP if by_pair[0].shape[0] % STEP == 0 else by_pair[0].shape[0]
+    count = by_pair[0].shape[0] // steps
+    cut = lambda a: pl.BlockSpec((count,) + a.shape[1:], lambda n: (n, 0, 0))
+    full = lambda a: pl.BlockSpec(a.shape, lambda n: (0, 0))
+    outs = [jax.ShapeDtypeStruct(by_pair[0].shape, BF16)] * pair_outs
+    sums = [jax.ShapeDtypeStruct(s, F32) for s in sum_outs]
+    return pl.pallas_call(
+        kernel,
+        grid=(steps,),
+        in_specs=[cut(a) for a in by_pair] + [full(a) for a in whole],
+        out_specs=[cut(a) for a in outs] + [full(a) for a in sums],
+        out_shape=outs + sums,
+        compiler_params=pltpu.CompilerParams(vmem_limit_bytes=GRANT),
+        name=name,
+    )(*by_pair, *whole)
+
+
+def outgoing_kernel(left_ref, right_ref, out_ref):
+    rows, chan, _, short, long = left_ref.shape
+    left = [left_ref[r].reshape(chan * short, long) for r in range(rows)]
+    right = [right_ref[r].reshape(chan * short, long) for r in range(rows)]
+    part = chan // rows
+    for r in range(rows):
+        for q in range(rows):
+            product = mm(right[q], left[r], TN).astype(BF16)
+            out_ref[r, q * part : (q + 1) * part] = product.reshape(part, 1, short, long)
+
+
+def backward_kernel(grad_ref, left_ref, right_ref, left_grad_ref, right_grad_ref):
+    rows, chan, _, short, long = left_ref.shape
+    load = lambda ref: [ref[r].reshape(chan * short, long) for r in range(rows)]
+    grad, left, right = load(grad_ref), load(left_ref), load(right_ref)
+    for r in range(rows):
+        total = sum(mm(right[q], grad[r][q * long : (q + 1) * long]) for q in range(rows))
+        left_grad_ref[r] = total.astype(BF16).reshape(chan, 1, short, long)
+        total = sum(mm(left[q], grad[q][r * long : (r + 1) * long], NT) for q in range(rows))
+        right_grad_ref[r] = total.astype(BF16).reshape(chan, 1, short, long)
+
+
+def incoming_kernel(left_ref, right_ref, out_ref):
+    rows, chan, _, short, long = left_ref.shape
+    load = lambda ref: [ref[r].reshape(chan * short, long) for r in range(rows)]
+    left, right = load(left_ref), load(right_ref)
+    for r in range(rows):
+        total = sum(mm(right[q], left[q][r * long : (r + 1) * long], NT) for q in range(rows))
+        out_ref[r] = total.astype(BF16).reshape(chan, 1, short, long)
+
+
+def by_channel(kernel, slabs, outs, name):
+    rows, chan, per, short, long = slabs[0].shape
+    spec = pl.BlockSpec((rows, chan, 1, short, long), lambda n: (0, 0, n, 0, 0))
+    return pl.pallas_call(
+        kernel,
+        grid=(per,),
+        in_specs=[spec] * len(slabs),
+        out_specs=[spec] * outs,
+        out_shape=[jax.ShapeDtypeStruct(slabs[0].shape, BF16)] * outs,
+        compiler_params=pltpu.CompilerParams(vmem_limit_bytes=GRANT),
+        name=name,
+    )(*slabs)
+
+
+def exchange(values):
+    return lax.all_to_all(values, BOTH, split_axis=0, concat_axis=0, tiled=True)
+
+
+def few_shards(
+    rows, chan,
+    pair_rep, upstream, out_proj, out_gate, out_final, in_proj, in_gate, in_final, out_drop, in_drop
+):
+    long, short, channels = pair_rep.shape
+    hidden = out_final.shape[0]
+    per = hidden // (rows * chan)
+    tokens = long * rows
+
+    def to_slab(values):
+        sent = exchange(jnp.swapaxes(values, 0, 1))
+        return sent.reshape(rows, chan, per, short, long)
+
+    def to_pairs(slab):
+        return jnp.swapaxes(exchange(slab.reshape(hidden, short, long)), 0, 1)
+
+    def column(mask):
+        return (mask.astype(F32) / keep_rate)[:, :, None]
+
+    pair = jnp.transpose(pair_rep, (1, 2, 0))
+    up = jnp.transpose(upstream, (1, 2, 0))
+    out_proj_t, in_proj_t = out_proj.T, in_proj.T
+    left, right = pairwise(front_kernel, [pair], [out_proj_t], 2, [], "front")
+    left, right = to_slab(left), to_slab(right)
+    (triangle,) = by_channel(outgoing_kernel, [left, right], 1, "outgoing")
+    middle, tri_grad, pre_grad, left_two, right_two, grad_gate, grad_final = pairwise(
+        middle_kernel,
+        [to_pairs(triangle), pair, up, column(out_drop)],
+        [out_gate.T, out_final.T, out_final, in_proj_t],
+        5,
+        [out_gate.shape, out_final.shape],
+        "middle",
+    )
+    tri_grad = to_slab(tri_grad)
+    left_grad, right_grad = by_channel(backward_kernel, [tri_grad, left, right], 2, "backward")
+    left_two, right_two = to_slab(left_two), to_slab(right_two)
+    (tri_two,) = by_channel(incoming_kernel, [left_two, right_two], 1, "incoming")
+    grad_pair, grad_proj = pairwise(
+        back_kernel,
+        [pair, up, pre_grad, to_pairs(left_grad), to_pairs(right_grad)],
+        [out_proj_t, out_proj, out_gate],
+        1,
+        [out_proj.shape],
+        "back",
+    )
+    grads = jnp.concatenate([grad_proj, grad_gate, grad_final], 1)
+    grads = exchange(grads).reshape(rows * chan, -1, grads.shape[1])
+    grads = lax.all_gather(jnp.sum(grads, 0) / tokens, BOTH, axis=0, tiled=True)
+    (final_pair,) = pairwise(
+        final_kernel,
+        [to_pairs(tri_two), middle, column(in_drop)],
+        [in_gate.T, in_final.T],
+        1,
+        [],
+        "final",
+    )
+    wide = out_proj.shape[1]
+    return (
+        jnp.transpose(final_pair, (2, 0, 1)),
+        jnp.transpose(grad_pair, (2, 0, 1)),
+        grads[:, :wide],
+        grads[:, wide : wide + channels],
+        grads[:, wide + channels :],
+    )
 
 
 def layer_norm(values, along):
@@ -160,6 +409,9 @@
 
 
 def solution(mesh):
+    rows, chan = mesh.shape["rows"], mesh.shape["chan"]
+    few = H % (rows * chan) == 0 and chan % rows == 0 and N // rows >= 128 and N // chan >= 16
+    shard = functools.partial(few_shards, rows, chan) if few else shards
     in_specs = (
         P("rows", "chan", None),
         P("rows", "chan", None),
@@ -173,4 +425,4 @@
         P("chan", None),
     )
     out_specs = (P("rows", "chan", None), P("rows", "chan", None), P(), P(), P())
-    return jax.shard_map(shards, mesh=mesh, in_specs=in_specs, out_specs=out_specs, check_vma=False)
+    return jax.shard_map(shard, mesh=mesh, in_specs=in_specs, out_specs=out_specs, check_vma=False)

time: 960 us -> 592 us (0.62); the launches traced: 949 us -> 590 us
  local copies, waits for them, and re-layouts: 207 us -> 65 us
  other arithmetic: 106 us -> 0.13 us
  blocking collectives: 210 us -> 148 us
  matrix products: 58.3 us -> 0 us
  Pallas kernels: 0 us -> 48.3 us
  starting transfers between devices: 54.4 us -> 29.5 us
  between operations: 14.6 us -> 1.05 us
    all_to_all x7 -> x8, waiting for transfers between devices: 137 us -> 298 us  [exchange(): return lax.all_to_all(values, BOTH, split_axis=0, concat_axis=0, tiled=True)]
    psum x1 -> x0, waiting for transfers between devices: 139 us -> none  [shards(): summed = lax.psum((grad_proj, grad_gate, grad_final), ('rows', 'chan'))]
    convert_element_type x15 -> x0, local copies, waits for them, and re-layouts: 129 us -> none  [the longest x5 52.8 us: finish(): triangle.reshape(hidden, -1).astype(jnp.float32)]
    all_to_all x4 -> x2, blocking collectives: 210 us -> 105 us  [exchange(): return lax.all_to_all(values, BOTH, split_axis=0, concat_axis=0, tiled=True)]
    dot_general x16 -> x0, matrix products: 58.3 us -> none  [the longest x2 7.57 us: front(): jnp.dot(normed, gate_w, preferred_element_type=jnp.float32)]
    pallas_call x0 -> x7, Pallas kernels: none -> 48.3 us  [the longest x4 35.5 us: pairwise(): pl.pallas_call(kernel, grid=(steps,), in_specs=[cut(a) for a in by_pair]...]
    reduce_sum x10 -> x1, other arithmetic: 44.2 us -> 0.08 us  [few_shards(): grads = lax.all_gather(jnp.sum(grads, 0) / tokens, BOTH, axis=0, tiled=True)]
    all_gather x0 -> x1, blocking collectives: none -> 42.8 us  [few_shards(): grads = lax.all_gather(jnp.sum(grads, 0) / tokens, BOTH, axis=0, tiled=True)]
  transfers between devices with their start and end apart: 11 -> 8, of which waited for: 7 -> 7; matrix products, arithmetic and copies ran while one was open for 11% -> 6% of each run, Pallas kernels for 0% -> 5%
where the time goes in v1:
time: 592 us; the launch traced here: 590 us
  waiting for transfers between devices  298 us (50%)
  blocking collectives  148 us (25%)
  local copies, waits for them, and re-layouts  65 us (11%)
  Pallas kernels  48.3 us (8%)
  starting transfers between devices  29.5 us (5%)
    all_to_all x8, waiting for transfers between devices, exchange(): return lax.all_to_all(values, BOTH, split_axis=0, concat_axis=0, tiled=True)  298 us
    all_to_all x2, blocking collectives, exchange(): return lax.all_to_all(values, BOTH, split_axis=0, concat_axis=0, tiled=True)  105 us
    all_gather x1, blocking collectives, few_shards(): grads = lax.all_gather(jnp.sum(grads, 0) / tokens, BOTH, axis=0, tiled=True)  42.8 us
    pallas_call x4, Pallas kernels, pairwise(): pl.pallas_call(kernel, grid=(steps,), in_specs=[cut(a) for a in by_pair]...  35.5 us
    unnamed x65, local copies, waits for them, and re-layouts  33.1 us
    all_to_all x8, starting transfers between devices, exchange(): return lax.all_to_all(values, BOTH, split_axis=0, concat_axis=0, tiled=True)  29.5 us
    transpose x5, local copies, waits for them, and re-layouts, to_slab(): sent = exchange(jnp.swapaxes(values, 0, 1))  17.2 us
    pallas_call x3, Pallas kernels, by_channel(): pl.pallas_call(kernel, grid=(per,), in_specs=[spec] * len(slabs), out_spe...  12.9 us
  transfers between devices with their start and end apart: 8, of which 7 were waited for; matrix products, arithmetic and copies ran while one was open for 6% of the time, Pallas kernels for 5%

profile of v1, /device:TPU:0, one launch (start us, length us, event | category | flops | bytes accessed | tf_op | source)
XLA Modules:
  0.0 590.5 jit_solution(16052072443438438440)
XLA Ops:
  0.6 3.0 copy.76
  3.8 4.2 front.1
  11.8 7.3 %all-to-all-start = ((bf16[128,32,256]{2,1,0:T(8,128)(2,1)}), bf16[128,32,256]{2,1,0:T(8,128)(2,1)S(1)}, u32[]{:S(2)}, u32[]{:S(2)}) async-start(bf16[128,32,256]{2,1,0:T(8,128)(2,1)} %copy.78), calls=%async_computation | async-start | bytes 4194304 | tf_op jit(solution)/shard_map/all_to_all | solution.py:193
  19.1 4.1 copy.79
  23.2 46.0 %all-to-all-done = bf16[128,32,256]{2,1,0:T(8,128)(2,1)S(1)} async-done(((bf16[128,32,256]{2,1,0:T(8,128)(2,1)}), bf16[128,32,256]{2,1,0:T(8,128)(2,1)S(1)}, u32[]{:S(2)}, u32[]{:S(2)}) %all-to-all-start) | async-done | bytes 2097184 | tf_op jit(solution)/shard_map/all_to_all | solution.py:193
  69.2 52.4 %all_to_all.54 = bf16[128,32,256]{2,1,0:T(8,128)(2,1)S(1)} all-to-all(bf16[128,32,256]{2,1,0:T(8,128)(2,1)} %copy.79), channel_id=1, replica_groups=mesh['rows'=2,'chan'=16] {'rows','chan'}, dimensions={0} | all-to-all | bytes 4194304 | tf_op jit(solution)/shard_map/all_to_all | solution.py:193
  125.3 3.5 all-to-all-start.2
  128.8 4.3 copy.81
  135.5 43.4 %all-to-all-done.2 = bf16[128,32,256]{2,1,0:T(8,128)(2,1)} async-done(((bf16[128,32,256]{2,1,0:T(8,128)(2,1)}), bf16[128,32,256]{2,1,0:T(8,128)(2,1)}, u32[]{:S(2)}, u32[]{:S(2)}) %all-to-all-start.2) | async-done | bytes 2097184 | tf_op jit(solution)/shard_map/all_to_all | solution.py:193
  178.9 2.8 copy.104
  181.7 14.6 %middle.1 = (bf16[32,128,256]{2,1,0:T(8,128)(2,1)S(1)}, bf16[32,128,256]{2,1,0:T(8,128)(2,1)S(1)}, bf16[32,128,256]{2,1,0:T(8,128)(2,1)S(1)}, bf16[32,128,256]{2...) custom-call(bf16[32,128,256]{2,1,0:T(8,128)(2,1)S(1)} %bitcast.52, ...), custom_call_target="tpu_custom_call" | custom-call | tf_op jit(solution)/shard_map/middle/pallas_call | solution.py:136
  204.1 3.5 all-to-all-start.6
  207.6 4.1 copy.86
  211.7 46.1 %all-to-all-done.6 = bf16[128,32,256]{2,1,0:T(8,128)(2,1)} async-done(((bf16[128,32,256]{2,1,0:T(8,128)(2,1)}), bf16[128,32,256]{2,1,0:T(8,128)(2,1)}, u32[]{:S(2)}, u32[]{:S(2)}) %all-to-all-start.6) | async-done | bytes 2097184 | tf_op jit(solution)/shard_map/all_to_all | solution.py:193
  257.7 3.7 all-to-all-start.3
  261.4 4.1 copy.87
  265.5 45.9 %all-to-all-done.3 = bf16[128,32,256]{2,1,0:T(8,128)(2,1)} async-done(((bf16[128,32,256]{2,1,0:T(8,128)(2,1)}), bf16[128,32,256]{2,1,0:T(8,128)(2,1)}, u32[]{:S(2)}, u32[]{:S(2)}) %all-to-all-start.3) | async-done | bytes 2097184 | tf_op jit(solution)/shard_map/all_to_all | solution.py:193
  311.3 3.5 all-to-all-start.4
  316.4 5.5 backward.1
  323.2 41.8 %all-to-all-done.4 = bf16[128,32,256]{2,1,0:T(8,128)(2,1)} async-done(((bf16[128,32,256]{2,1,0:T(8,128)(2,1)}), bf16[128,32,256]{2,1,0:T(8,128)(2,1)}, u32[]{:S(2)}, u32[]{:S(2)}) %all-to-all-start.4) | async-done | bytes 2097184 | tf_op jit(solution)/shard_map/all_to_all | solution.py:193
  365.0 53.1 %all_to_all.55 = bf16[128,32,256]{2,1,0:T(8,128)(2,1)} all-to-all(bf16[128,32,256]{2,1,0:T(8,128)(2,1)} %bitcast.61), channel_id=1, replica_groups=mesh['rows'=2,'chan'=16] {'rows','chan'}, dimensions={0} | all-to-all | bytes 4194304 | tf_op jit(solution)/shard_map/all_to_all | solution.py:193
  420.8 5.0 incoming.1
  425.8 45.1 %all-to-all-done.7 = bf16[128,32,256]{2,1,0:T(8,128)(2,1)S(1)} async-done(((bf16[128,32,256]{2,1,0:T(8,128)(2,1)}), bf16[128,32,256]{2,1,0:T(8,128)(2,1)S(1)}, u32[]{:S(2)}, u32[]{:S(2)}) %all-to-all-start.7) | async-done | bytes 2097184 | tf_op jit(solution)/shard_map/all_to_all | solution.py:193
  472.3 2.7 all-to-all-start.5
  475.1 2.9 copy.101
  480.2 12.8 %back.1 = (bf16[32,128,256]{2,1,0:T(8,128)(2,1)S(1)}, f32[128,512]{1,0:T(8,128)S(1)}) custom-call(bf16[32,128,256]{2,1,0:T(8,128)(2,1)S(1)} %bitcast.44, bf16[32,128,256]{2,1,0:T(8,128)(2,1)S(1)} %bitcast.50, bf16[32,128,256]{2,1,0:T(8,128)(2,1)S(1)} %copy-done.15, bf16[32,128,256]{2,1,0:T(8,128)(2,1)S(1)} %bitcast.54, bf16[32,128,256]{2,1,0:T(8,128)(2,1)S(1)} %bitcast.53, ...), custom_call_target="tpu_custom_call" | custom-call | tf_op jit(solution)/shard_map/back/pallas_call | solution.py:136
  495.3 30.0 %all-to-all-done.5 = bf16[128,32,256]{2,1,0:T(8,128)(2,1)S(1)} async-done(((bf16[128,32,256]{2,1,0:T(8,128)(2,1)}), bf16[128,32,256]{2,1,0:T(8,128)(2,1)S(1)}, u32[]{:S(2)}, u32[]{:S(2)}) %all-to-all-start.5) | async-done | bytes 2097184 | tf_op jit(solution)/shard_map/all_to_all | solution.py:193
  528.8 4.5 copy.96
  533.3 2.9 copy.103
  536.2 4.0 final.1
  541.5 4.5 copy.95
  546.1 42.8 %all-gather = f32[32,4,768]{2,1,0:T(4,128)S(1)} all-gather(f32[1,4,768]{2,1,0:T(4,128)S(1)} %multiply_bitcast_fusion.2), channel_id=1, replica_groups=mesh['rows'=2,'chan'=16] {'rows','chan'}, dimensions={0}, use_global_device_ids=true | all-gather | bytes 405504 | tf_op jit(solution)/shard_map/all_gather | solution.py:243
  (78 shorter events, 35.7 us)
Async XLA Ops:
  0.6 3.0 copy-start.16
  3.7 8.1 %copy-start = (bf16[256,32,128]{0,2,1:T(8,128)(2,1)}, bf16[256,32,128]{0,2,1:T(8,128)(2,1)S(1)}, u32[]{:S(2)}) copy-start(bf16[256,32,128]{0,2,1:T(8,128)(2,1)S(1)} %copy.76) | copy-start | bytes 6291460
  8.0 1.3 copy-start.11
  11.8 57.4 %all-to-all-start = ((bf16[128,32,256]{2,1,0:T(8,128)(2,1)}), bf16[128,32,256]{2,1,0:T(8,128)(2,1)S(1)}, u32[]{:S(2)}, u32[]{:S(2)}) async-start(bf16[128,32,256]{2,1,0:T(8,128)(2,1)} %copy.78), calls=%async_computation | async-start | bytes 4194304 | tf_op jit(solution)/shard_map/all_to_all | solution.py:193
  121.6 2.4 copy-start.2
  124.0 1.3 copy-start.5
  125.3 53.6 %all-to-all-start.2 = ((bf16[128,32,256]{2,1,0:T(8,128)(2,1)}), bf16[128,32,256]{2,1,0:T(8,128)(2,1)}, u32[]{:S(2)}, u32[]{:S(2)}) async-start(bf16[128,32,256]{2,1,0:T(8,128)(2,1)} %bitcast.51), calls=%async_computation.2 | async-start | bytes 4194304 | tf_op jit(solution)/shard_map/all_to_all | solution.py:193
  128.8 4.3 copy-start.25
  133.1 2.1 copy-start.22
  133.1 2.2 copy-start.18
  133.1 2.3 copy-start.17
  198.9 1.3 copy-start.12
  200.2 1.4 copy-start.14
  204.1 53.6 %all-to-all-start.6 = ((bf16[128,32,256]{2,1,0:T(8,128)(2,1)}), bf16[128,32,256]{2,1,0:T(8,128)(2,1)}, u32[]{:S(2)}, u32[]{:S(2)}) async-start(bf16[128,32,256]{2,1,0:T(8,128)(2,1)} %copy.92), calls=%async_computation.6 | async-start | bytes 4194304 | tf_op jit(solution)/shard_map/all_to_all | solution.py:193
  257.7 53.6 %all-to-all-start.3 = ((bf16[128,32,256]{2,1,0:T(8,128)(2,1)}), bf16[128,32,256]{2,1,0:T(8,128)(2,1)}, u32[]{:S(2)}, u32[]{:S(2)}) async-start(bf16[128,32,256]{2,1,0:T(8,128)(2,1)} %copy.86), calls=%async_computation.3 | async-start | bytes 4194304 | tf_op jit(solution)/shard_map/all_to_all | solution.py:193
  311.3 53.6 %all-to-all-start.4 = ((bf16[128,32,256]{2,1,0:T(8,128)(2,1)}), bf16[128,32,256]{2,1,0:T(8,128)(2,1)}, u32[]{:S(2)}, u32[]{:S(2)}) async-start(bf16[128,32,256]{2,1,0:T(8,128)(2,1)} %copy.87), calls=%async_computation.4 | async-start | bytes 4194304 | tf_op jit(solution)/shard_map/all_to_all | solution.py:193
  314.8 1.6 copy-start.3
  418.0 52.9 %all-to-all-start.7 = ((bf16[128,32,256]{2,1,0:T(8,128)(2,1)}), bf16[128,32,256]{2,1,0:T(8,128)(2,1)S(1)}, u32[]{:S(2)}, u32[]{:S(2)}) async-start(bf16[128,32,256]{2,1,0:T(8,128)(2,1)} %bitcast.25), calls=%async_computation.7 | async-start | bytes 4194304 | tf_op jit(solution)/shard_map/all_to_all | solution.py:193
  470.9 1.4 copy-start.20
  472.3 52.9 %all-to-all-start.5 = ((bf16[128,32,256]{2,1,0:T(8,128)(2,1)}), bf16[128,32,256]{2,1,0:T(8,128)(2,1)S(1)}, u32[]{:S(2)}, u32[]{:S(2)}) async-start(bf16[128,32,256]{2,1,0:T(8,128)(2,1)} %bitcast.17), calls=%async_computation.5 | async-start | bytes 4194304 | tf_op jit(solution)/shard_map/all_to_all | solution.py:193
  475.1 2.9 copy-start.21
  475.1 4.1 copy-start.15
  478.0 1.6 copy-start.1
  478.0 2.2 copy-start.4
  493.0 1.4 copy-start.8
  494.4 33.5 %copy-start.26 = (s32[32,128]{1,0:T(8,128)S(1)}, s32[32,128]{1,0:T(8,128)}, u32[]{:S(2)}) copy-start(s32[32,128]{1,0:T(8,128)} %param.19) | copy-start | bytes 49156
  494.4 34.2 %copy-start.23 = (bf16[128,128]{1,0:T(8,128)(2,1)S(1)}, bf16[128,128]{1,0:T(8,128)(2,1)}, u32[]{:S(2)}) copy-start(bf16[128,128]{1,0:T(8,128)(2,1)} %param.16) | copy-start | bytes 98308
  494.4 34.3 %copy-start.24 = (bf16[128,128]{1,0:T(8,128)(2,1)S(1)}, bf16[128,128]{1,0:T(8,128)(2,1)}, u32[]{:S(2)}) copy-start(bf16[128,128]{1,0:T(8,128)(2,1)} %param.17) | copy-start | bytes 98308
  525.2 2.6 copy-start.19
  525.2 20.8 %all-to-all-start.9 = ((f32[32,4,768]{2,1,0:T(4,128)}), f32[32,4,768]{2,1,0:T(4,128)S(1)}, u32[]{:S(2)}, u32[]{:S(2)}) async-start(f32[32,4,768]{2,1,0:T(4,128)} %all_to_all.42), calls=%async_computation.9 | async-start | bytes 786432 | tf_op jit(solution)/shard_map/all_to_all | solution.py:193
  533.3 2.9 copy-start.13
  540.2 1.4 copy-start.6
  (3 other events, 3.9 us)

commit v2 on v1

--- a/solution.py
+++ b/solution.py
@@ -144,47 +144,162 @@
     )(*by_pair, *whole)
 
 
-def outgoing_kernel(left_ref, right_ref, out_ref):
-    rows, chan, _, short, long = left_ref.shape
-    left = [left_ref[r].reshape(chan * short, long) for r in range(rows)]
-    right = [right_ref[r].reshape(chan * short, long) for r in range(rows)]
+MESH = pl.DeviceIdType.MESH
+
+
+def crossed(a, b, size):
+    total, bit = 0, 1
+    while bit < size:
+        total = total + bit * ((a // bit + b // bit) % 2)
+        bit *= 2
+    return total
+
+
+def partner(step, rows, chan):
+    row = crossed(lax.axis_index("rows"), step // chan, rows)
+    col = crossed(lax.axis_index("chan"), step % chan, chan)
+    return row, col
+
+
+def greet(rows, chan):
+    barrier = pltpu.get_barrier_semaphore()
+
+    def signal(step, carry):
+        pl.semaphore_signal(
+            barrier, inc=1, device_id=partner(step, rows, chan), device_id_type=MESH
+        )
+        return carry
+
+    lax.fori_loop(1, rows * chan, signal, 0)
+    pl.semaphore_wait(barrier, rows * chan - 1)
+
+
+def remote(rows, chan, src, dst, send, recv, at, step):
+    row, col = partner(step, rows, chan)
+    me = lax.axis_index("rows") * chan + lax.axis_index("chan")
+    return pltpu.make_async_remote_copy(
+        src.at[row * chan + col],
+        dst.at[me],
+        send.at[at, step],
+        recv.at[at, step],
+        device_id=(row, col),
+        device_id_type=MESH,
+    )
+
+
+def local(chan, src, dst, send, at):
+    me = lax.axis_index("rows") * chan + lax.axis_index("chan")
+    return pltpu.make_async_copy(src.at[me], dst.at[me], send.at[at, 0])
+
+
+def send_all(rows, chan, src, dst, send, recv, at):
+    def body(step, carry):
+        remote(rows, chan, src, dst, send, recv, at, step).start()
+        return carry
+
+    local(chan, src, dst, send, at).start()
+    lax.fori_loop(1, rows * chan, body, 0)
+
+
+def wait_all(rows, chan, src, dst, send, recv, at):
+    def body(step, carry):
+        remote(rows, chan, src, dst, send, recv, at, step).wait()
+        return carry
+
+    local(chan, src, dst, send, at).wait()
+    lax.fori_loop(1, rows * chan, body, 0)
+
+
+def planes(ref, h, rows):
+    chan, (_, short, long) = ref.shape[0] // rows, ref.shape[1:]
+    return [ref[r * chan : (r + 1) * chan, h].reshape(chan * short, long) for r in range(rows)]
+
+
+def outgoing_kernel(
+    rows, chan, left_in, right_in, left_ref, right_ref, tri_ref, product_ref, send, recv
+):
+    per, short, long = left_ref.shape[1:]
     part = chan // rows
-    for r in range(rows):
-        for q in range(rows):
-            product = mm(right[q], left[r], TN).astype(BF16)
-            out_ref[r, q * part : (q + 1) * part] = product.reshape(part, 1, short, long)
-
-
-def backward_kernel(grad_ref, left_ref, right_ref, left_grad_ref, right_grad_ref):
-    rows, chan, _, short, long = left_ref.shape
-    load = lambda ref: [ref[r].reshape(chan * short, long) for r in range(rows)]
-    grad, left, right = load(grad_ref), load(left_ref), load(right_ref)
-    for r in range(rows):
-        total = sum(mm(right[q], grad[r][q * long : (q + 1) * long]) for q in range(rows))
-        left_grad_ref[r] = total.astype(BF16).reshape(chan, 1, short, long)
-        total = sum(mm(left[q], grad[q][r * long : (r + 1) * long], NT) for q in range(rows))
-        right_grad_ref[r] = total.astype(BF16).reshape(chan, 1, short, long)
-
-
-def incoming_kernel(left_ref, right_ref, out_ref):
-    rows, chan, _, short, long = left_ref.shape
-    load = lambda ref: [ref[r].reshape(chan * short, long) for r in range(rows)]
-    left, right = load(left_ref), load(right_ref)
-    for r in range(rows):
-        total = sum(mm(right[q], left[q][r * long : (r + 1) * long], NT) for q in range(rows))
-        out_ref[r] = total.astype(BF16).reshape(chan, 1, short, long)
-
-
-def by_channel(kernel, slabs, outs, name):
-    rows, chan, per, short, long = slabs[0].shape
-    spec = pl.BlockSpec((rows, chan, 1, short, long), lambda n: (0, 0, n, 0, 0))
+    moves = [(left_in, left_ref), (right_in, right_ref), (product_ref, tri_ref)]
+    greet(rows, chan)
+    for at in range(2):
+        send_all(rows, chan, *moves[at], send, recv, at)
+    for at in range(2):
+        wait_all(rows, chan, *moves[at], send, recv, at)
+
+    def body(h, carry):
+        left, right = planes(left_ref, h, rows), planes(right_ref, h, rows)
+        for r in range(rows):
+            for q in range(rows):
+                product = mm(right[q], left[r], TN).astype(BF16)
+                first = r * chan + q * part
+                product_ref[first : first + part, h] = product.reshape(part, short, long)
+        return carry
+
+    lax.fori_loop(0, per, body, 0)
+    send_all(rows, chan, *moves[2], send, recv, 2)
+    wait_all(rows, chan, *moves[2], send, recv, 2)
+
+
+def backward_kernel(
+    rows, chan, grad_in, left_two_in, right_two_in, left_ref, right_ref,
+    left_out, right_out, tri_two_ref,
+    grad_ref, left_two_ref, right_two_ref, left_grad_ref, right_grad_ref, send, recv,
+):
+    per, short, long = left_ref.shape[1:]
+    moves = [
+        (grad_in, grad_ref),
+        (left_two_in, left_two_ref),
+        (right_two_in, right_two_ref),
+        (left_grad_ref, left_out),
+        (right_grad_ref, right_out),
+    ]
+    greet(rows, chan)
+    for at in range(3):
+        send_all(rows, chan, *moves[at], send, recv, at)
+    wait_all(rows, chan, *moves[0], send, recv, 0)
+
+    def back(h, carry):
+        grad, left, right = (planes(ref, h, rows) for ref in (grad_ref, left_ref, right_ref))
+        for r in range(rows):
+            at = slice(r * chan, (r + 1) * chan)
+            total = sum(mm(right[q], grad[r][q * long : (q + 1) * long]) for q in range(rows))
+            left_grad_ref[at, h] = total.astype(BF16).reshape(chan, short, long)
+            total = sum(mm(left[q], grad[q][r * long : (r + 1) * long], NT) for q in range(rows))
+            right_grad_ref[at, h] = total.astype(BF16).reshape(chan, short, long)
+        return carry
+
+    lax.fori_loop(0, per, back, 0)
+    for at in (3, 4):
+        send_all(rows, chan, *moves[at], send, recv, at)
+    for at in (1, 2):
+        wait_all(rows, chan, *moves[at], send, recv, at)
+
+    def two(h, carry):
+        left, right = planes(left_two_ref, h, rows), planes(right_two_ref, h, rows)
+        for r in range(rows):
+            total = sum(mm(right[q], left[q][r * long : (r + 1) * long], NT) for q in range(rows))
+            tri_two_ref[r * chan : (r + 1) * chan, h] = total.astype(BF16).reshape(chan, short, long)
+        return carry
+
+    lax.fori_loop(0, per, two, 0)
+    for at in (3, 4):
+        wait_all(rows, chan, *moves[at], send, recv, at)
+
+
+def fused(kernel, rows, chan, slabs, outs, held, moves, number, name):
+    vmem = pl.BlockSpec(memory_space=pltpu.VMEM)
+    shape = slabs[0].shape
     return pl.pallas_call(
-        kernel,
-        grid=(per,),
-        in_specs=[spec] * len(slabs),
-        out_specs=[spec] * outs,
-        out_shape=[jax.ShapeDtypeStruct(slabs[0].shape, BF16)] * outs,
-        compiler_params=pltpu.CompilerParams(vmem_limit_bytes=GRANT),
+        functools.partial(kernel, rows, chan),
+        in_specs=[vmem] * len(slabs),
+        out_specs=[vmem] * outs,
+        out_shape=[jax.ShapeDtypeStruct(shape, BF16)] * outs,
+        scratch_shapes=[pltpu.VMEM(shape, BF16)] * held
+        + [pltpu.SemaphoreType.DMA((moves, rows * chan))] * 2,
+        compiler_params=pltpu.CompilerParams(
+            collective_id=number, has_side_effects=True, vmem_limit_bytes=GRANT
+        ),
         name=name,
     )(*slabs)
 
@@ -203,11 +318,10 @@
     tokens = long * rows
 
     def to_slab(values):
-        sent = exchange(jnp.swapaxes(values, 0, 1))
-        return sent.reshape(rows, chan, per, short, long)
+        return jnp.swapaxes(values, 0, 1).reshape(rows * chan, per, short, long)
 
     def to_pairs(slab):
-        return jnp.swapaxes(exchange(slab.reshape(hidden, short, long)), 0, 1)
+        return jnp.swapaxes(slab.reshape(hidden, short, long), 0, 1)
 
     def column(mask):
         return (mask.astype(F32) / keep_rate)[:, :, None]
@@ -216,8 +330,9 @@
     up = jnp.transpose(upstream, (1, 2, 0))
     out_proj_t, in_proj_t = out_proj.T, in_proj.T
     left, right = pairwise(front_kernel, [pair], [out_proj_t], 2, [], "front")
-    left, right = to_slab(left), to_slab(right)
-    (triangle,) = by_channel(outgoing_kernel, [left, right], 1, "outgoing")
+    left, right, triangle = fused(
+        outgoing_kernel, rows, chan, [to_slab(left), to_slab(right)], 3, 1, 3, 1, "outgoing"
+    )
     middle, tri_grad, pre_grad, left_two, right_two, grad_gate, grad_final = pairwise(
         middle_kernel,
         [to_pairs(triangle), pair, up, column(out_drop)],
@@ -226,10 +341,11 @@
         [out_gate.shape, out_final.shape],
         "middle",
     )
-    tri_grad = to_slab(tri_grad)
-    left_grad, right_grad = by_channel(backward_kernel, [tri_grad, left, right], 2, "backward")
-    left_two, right_two = to_slab(left_two), to_slab(right_two)
-    (tri_two,) = by_channel(incoming_kernel, [left_two, right_two], 1, "incoming")
+    slabs = [to_slab(tri_grad), to_slab(left_two), to_slab(right_two), left, right]
+    left_grad, right_grad, tri_two = fused(
+        backward_kernel, rows, chan, slabs, 3, 5, 5, 2, "backward"
+    )
+    tri_two = exchange(tri_two)
     grad_pair, grad_proj = pairwise(
         back_kernel,
         [pair, up, pre_grad, to_pairs(left_grad), to_pairs(right_grad)],
@@ -239,8 +355,9 @@
         "back",
     )
     grads = jnp.concatenate([grad_proj, grad_gate, grad_final], 1)
-    grads = exchange(grads).reshape(rows * chan, -1, grads.shape[1])
-    grads = lax.all_gather(jnp.sum(grads, 0) / tokens, BOTH, axis=0, tiled=True)
+    grads = jnp.sum(exchange(grads).reshape(rows * chan, per, -1), 0) / tokens
+    grads = exchange(jnp.broadcast_to(grads[None], (rows * chan,) + grads.shape))
+    grads = grads.reshape(hidden, -1)
     (final_pair,) = pairwise(
         final_kernel,
         [to_pairs(tri_two), middle, column(in_drop)],
@@ -410,7 +527,8 @@
 
 def solution(mesh):
     rows, chan = mesh.shape["rows"], mesh.shape["chan"]
-    few = H % (rows * chan) == 0 and chan % rows == 0 and N // rows >= 128 and N // chan >= 16
+    few = H % (rows * chan) == 0 and chan % rows == 0 and rows & (rows - 1) == 0 and chan & (chan - 1) == 0
+    few = few and N // rows >= 128 and N // chan >= 16
     shard = functools.partial(few_shards, rows, chan) if few else shards
     in_specs = (
         P("rows", "chan", None),

time: 592 us -> 560 us (0.946)
  Pallas kernels: 48.3 us -> 438 us
  waiting for transfers between devices: 298 us -> 44.5 us
  blocking collectives: 148 us -> 34.7 us
  local copies, waits for them, and re-layouts: 65 us -> 37.6 us
  starting transfers between devices: 29.5 us -> 3.48 us
    pallas_call x3 -> x2, Pallas kernels: 12.9 us -> 403 us  [fused(): pl.pallas_call(functools.partial(kernel, rows, chan), in_specs=[vmem] * l...]
    all_to_all x8 -> x1, waiting for transfers between devices: 298 us -> 44.5 us  [exchange(): return lax.all_to_all(values, BOTH, split_axis=0, concat_axis=0, tiled=True)]
    all_to_all x2, blocking collectives: 105 us -> 34.7 us  [exchange(): return lax.all_to_all(values, BOTH, split_axis=0, concat_axis=0, tiled=True)]
    all_gather x1 -> x0, blocking collectives: 42.8 us -> none  [few_shards(): grads = lax.all_gather(jnp.sum(grads, 0) / tokens, BOTH, axis=0, tiled=True)]
    all_to_all x8 -> x1, starting transfers between devices: 29.5 us -> 3.48 us  [exchange(): return lax.all_to_all(values, BOTH, split_axis=0, concat_axis=0, tiled=True)]
    unnamed x65 -> x42, local copies, waits for them, and re-layouts: 33.1 us -> 21 us
    all_to_all x5 -> x1, local copies, waits for them, and re-layouts: 10.6 us -> 0.11 us  [exchange(): return lax.all_to_all(values, BOTH, split_axis=0, concat_axis=0, tiled=True)]
    transpose x5 -> x6, local copies, waits for them, and re-layouts: 17.2 us -> 8.26 us  [the longest x5 5.88 us: to_slab(): return jnp.swapaxes(values, 0, 1).reshape(rows * chan, per, short, long)]
  transfers between devices with their start and end apart: 8 -> 1, of which waited for: 7 -> 1; matrix products, arithmetic and copies ran while one was open for 6% -> 1% of each run, Pallas kernels for 5% -> 0%
where the time goes in v2:
time: 560 us; the launch traced here: 559 us
  Pallas kernels  438 us (78%)
  waiting for transfers between devices  44.5 us (8%)
  local copies, waits for them, and re-layouts  37.6 us (7%)
  blocking collectives  34.7 us (6%)
    pallas_call x2, Pallas kernels, fused(): pl.pallas_call(functools.partial(kernel, rows, chan), in_specs=[vmem] * l...  403 us
    all_to_all x1, waiting for transfers between devices, exchange(): return lax.all_to_all(values, BOTH, split_axis=0, concat_axis=0, tiled=True)  44.5 us
    pallas_call x4, Pallas kernels, pairwise(): pl.pallas_call(kernel, grid=(steps,), in_specs=[cut(a) for a in by_pair]...  35.5 us
    all_to_all x2, blocking collectives, exchange(): return lax.all_to_all(values, BOTH, split_axis=0, concat_axis=0, tiled=True)  34.7 us
    unnamed x42, local copies, waits for them, and re-layouts  21 us
  transfers between devices with their start and end apart: 1, of which 1 were waited for; matrix products, arithmetic and copies ran while one was open for 1% of the time, Pallas kernels for 0%

profile of v2, /device:TPU:0, one launch (start us, length us, event | category | flops | bytes accessed | tf_op | source)
XLA Modules:
  0.0 559.5 jit_solution(8432180775237009087)
XLA Ops:
  0.6 3.0 copy.55
  3.7 0.1 copy.56
  3.8 4.2 front.1
  8.0 1.2 copy.57
  9.2 1.2 copy.58
  10.4 158.9 %outgoing.1 = (bf16[32,4,32,256]{3,2,1,0:T(8,128)(2,1)S(1)}, bf16[32,4,32,256]{3,2,1,0:T(8,128)(2,1)S(1)}, bf16[32,4,32,256]{3,2,1,0:T(8,128)(2,1)S(1)}) custom-call(bf16[32,4,32,256]{3,2,1,0:T(8,128)(2,1)S(1)} %bitcast.46, bf16[32,4,32,256]{3,2,1,0:T(8,128)(2,1)S(1)} %bitcast.47), custom_call_target="tpu_custom_call" | custom-call | tf_op jit(solution)/shard_map/outgoing/pallas_call | solution.py:293
  169.3 1.3 copy-done.4
  170.6 1.3 copy-done.5
  171.9 1.2 copy.85
  173.1 4.3 copy.60
  177.4 2.0 copy.64.drop_ref
  179.8 14.6 %middle.1 = (bf16[32,128,256]{2,1,0:T(8,128)(2,1)S(1)}, bf16[32,128,256]{2,1,0:T(8,128)(2,1)S(1)}, bf16[32,128,256]{2,1,0:T(8,128)(2,1)S(1)}, bf16[32,128,256]{2...) custom-call(bf16[32,128,256]{2,1,0:T(8,128)(2,1)S(1)} %bitcast.48, ...), custom_call_target="tpu_custom_call" | custom-call | tf_op jit(solution)/shard_map/middle/pallas_call | solution.py:136
  194.4 1.3 copy-done.6
  195.7 1.2 copy.65
  196.9 1.2 copy.66
  198.1 1.2 copy.67
  199.3 243.7 %backward.1 = (bf16[32,4,32,256]{3,2,1,0:T(8,128)(2,1)S(1)}, bf16[32,4,32,256]{3,2,1,0:T(8,128)(2,1)S(1)}, bf16[32,4,32,256]{3,2,1,0:T(8,128)(2,1)}) custom-call(bf16[32,4,32,256]{3,2,1,0:T(8,128)(2,1)S(1)} %bitcast.43, bf16[32,4,32,256]{3,2,1,0:T(8,128)(2,1)S(1)} %bitcast.44, bf16[32,4,32,256]{3,2,1,0:T(8,128)(2,1)S(1)} %bitcast.45, ...), custom_call_target="tpu_custom_call" | custom-call | tf_op jit(solution)/shard_map/backward/pallas_call | solution.py:293
  443.0 2.4 copy_bitcast_fusion
  445.4 12.8 %back.1 = (bf16[32,128,256]{2,1,0:T(8,128)(2,1)S(1)}, f32[128,512]{1,0:T(8,128)S(1)}) custom-call(bf16[32,128,256]{2,1,0:T(8,128)(2,1)S(1)} %bitcast.40, bf16[32,128,256]{2,1,0:T(8,128)(2,1)S(1)} %bitcast.42, bf16[32,128,256]{2,1,0:T(8,128)(2,1)S(1)} %get-tuple-element.32.pre_ref, bf16[32,128,256]{2,1,0:T(8,128)(2,1)S(1)} %get-tuple-element.57.left_ref, ...), custom_call_target="tpu_custom_call" | custom-call | tf_op jit(solution)/shard_map/back/pallas_call | solution.py:136
  458.3 19.4 %all_to_all.19 = f32[32,4,768]{2,1,0:T(4,128)S(1)} all-to-all(f32[32,4,768]{2,1,0:T(4,128)S(1)} %all_to_all.13), channel_id=1, replica_groups=mesh['rows'=2,'chan'=16] {'rows','chan'}, dimensions={0} | all-to-all | bytes 786432 | tf_op jit(solution)/shard_map/all_to_all | solution.py:308
  477.9 15.2 %all_to_all.20 = f32[32,4,768]{2,1,0:T(4,128)S(1)} all-to-all(f32[32,4,768]{2,1,0:T(4,128)S(1)} %broadcast_in_dim.14), channel_id=1, replica_groups=mesh['rows'=2,'chan'=16] {'rows','chan'}, dimensions={0} | all-to-all | bytes 786432 | tf_op jit(solution)/shard_map/all_to_all | solution.py:308
  493.2 3.5 all-to-all-start
  496.7 3.1 copy.75
  499.7 0.6 copy.71.drop_ref
  500.7 0.1 reshape.56
  500.9 0.7 slice.12
  501.6 0.7 fusion
  502.3 44.5 %all-to-all-done = bf16[32,4,32,256]{3,2,1,0:T(8,128)(2,1)} async-done(((bf16[32,4,32,256]{3,2,1,0:T(8,128)(2,1)}), bf16[32,4,32,256]{3,2,1,0:T(8,128)(2,1)}, u32[]{:S(2)}, u32[]{:S(2)}) %all-to-all-start) | async-done | bytes 2097184 | tf_op jit(solution)/shard_map/all_to_all | solution.py:308
  546.8 2.9 copy.84
  549.7 4.0 final.1
  553.7 1.3 copy-done.3
  555.0 4.5 copy.74
  (40 shorter events, 1.0 us)
Async XLA Ops:
  0.6 3.0 copy-start.8
  3.7 5.5 copy-start
  169.3 1.3 copy-start.4
  170.6 1.3 copy-start.5
  173.1 4.3 copy-start.14
  177.4 2.0 copy-start.11
  177.4 2.1 copy-start.10
  177.4 2.3 copy-start.9
  194.4 1.3 copy-start.6
  443.0 2.4 copy-start.1
  443.0 2.4 copy-start.2
  493.2 53.6 %all-to-all-start = ((bf16[32,4,32,256]{3,2,1,0:T(8,128)(2,1)}), bf16[32,4,32,256]{3,2,1,0:T(8,128)(2,1)}, u32[]{:S(2)}, u32[]{:S(2)}) async-start(bf16[32,4,32,256]{3,2,1,0:T(8,128)(2,1)} %get-tuple-element.30), calls=%async_computation | async-start | bytes 4194304 | tf_op jit(solution)/shard_map/all_to_all | solution.py:308
  496.6 3.1 copy-start.15
  499.7 0.8 copy-start.12
  499.7 0.9 copy-start.13
  546.8 2.9 copy-start.7
  553.7 1.3 copy-start.3

commit v3 on v2

--- a/solution.py
+++ b/solution.py
@@ -13,7 +13,6 @@
 epsilon = 1e-05
 keep_rate = 0.75
 
-BOTH = ("rows", "chan")
 STEP = 4
 GRANT = 40 * 1024 * 1024
 F32 = jnp.float32
@@ -82,41 +81,6 @@
         sides(normed_two, proj_two_ref[...], left_ref, right_ref, at)
 
 
-def back_kernel(
-    pair_ref, up_ref, pre_ref, left_ref, right_ref, proj_t_ref, proj_ref, gate_ref,
-    grad_ref, grad_proj_ref,
-):
-    @pl.when(pl.program_id(0) == 0)
-    def _():
-        grad_proj_ref[...] = jnp.zeros_like(grad_proj_ref)
-
-    hidden = proj_t_ref.shape[0] // 4
-    for at in range(pair_ref.shape[0]):
-        scaled, inv_std = norm_cols(pair_ref[at].astype(F32))
-        normed = scaled.astype(BF16)
-        projected = mm(proj_t_ref[...], normed)
-        left, right = left_ref[at].astype(F32), right_ref[at].astype(F32)
-        left_sig = jax.nn.sigmoid(projected[:hidden])
-        right_sig = jax.nn.sigmoid(projected[2 * hidden : 3 * hidden])
-        left_val, right_val = left * left_sig, right * right_sig
-        proj_grad = jnp.concatenate(
-            [
-                (left_val * projected[hidden : 2 * hidden] * (1.0 - left_sig)).astype(BF16),
-                left_val.astype(BF16),
-                (right_val * projected[3 * hidden :] * (1.0 - right_sig)).astype(BF16),
-                right_val.astype(BF16),
-            ],
-            0,
-        )
-        grad_proj_ref[...] += mm(normed, proj_grad, NT)
-        input_grad = mm(proj_ref[...], proj_grad) + mm(gate_ref[...], pre_ref[at])
-        first = jnp.mean(input_grad, axis=0, keepdims=True)
-        second = jnp.mean(input_grad * scaled, axis=0, keepdims=True)
-        grad_ref[at] = (
-            up_ref[at].astype(F32) + inv_std * (input_grad - first - scaled * second)
-        ).astype(BF16)
-
-
 def final_kernel(tri_ref, mid_ref, drop_ref, gate_ref, final_t_ref, out_ref):
     for at in range(tri_ref.shape[0]):
         middle = mid_ref[at].astype(F32)
@@ -304,8 +268,111 @@
     )(*slabs)
 
 
-def exchange(values):
-    return lax.all_to_all(values, BOTH, split_axis=0, concat_axis=0, tiled=True)
+def tail_kernel(
+    rows, chan,
+    tri_in, pair_ref, up_ref, pre_ref, left_ref, right_ref, proj_t_ref, proj_ref, gate_ref, rest_ref,
+    tri_ref, grad_ref, sums_ref,
+    total_ref, parts_ref, from_chan, held_ref, from_rows, mine_ref, send, recv, small_send, small_recv,
+):
+    hidden = proj_t_ref.shape[0] // 4
+    wide = proj_t_ref.shape[0]
+    row, col = lax.axis_index("rows"), lax.axis_index("chan")
+    tokens = rows * pair_ref.shape[2]
+    greet(rows, chan)
+    send_all(rows, chan, tri_in, tri_ref, send, recv, 0)
+    total_ref[...] = jnp.zeros_like(total_ref)
+
+    def back(at, carry):
+        scaled, inv_std = norm_cols(pair_ref[at].astype(F32))
+        normed = scaled.astype(BF16)
+        projected = mm(proj_t_ref[...], normed)
+        left, right = left_ref[at].astype(F32), right_ref[at].astype(F32)
+        left_sig = jax.nn.sigmoid(projected[:hidden])
+        right_sig = jax.nn.sigmoid(projected[2 * hidden : 3 * hidden])
+        left_val, right_val = left * left_sig, right * right_sig
+        proj_grad = jnp.concatenate(
+            [
+                (left_val * projected[hidden : 2 * hidden] * (1.0 - left_sig)).astype(BF16),
+                left_val.astype(BF16),
+                (right_val * projected[3 * hidden :] * (1.0 - right_sig)).astype(BF16),
+                right_val.astype(BF16),
+            ],
+            0,
+        )
+        total_ref[...] += mm(normed, proj_grad, NT)
+        input_grad = mm(proj_ref[...], proj_grad) + mm(gate_ref[...], pre_ref[at])
+        first = jnp.mean(input_grad, axis=0, keepdims=True)
+        second = jnp.mean(input_grad * scaled, axis=0, keepdims=True)
+        grad_ref[at] = (
+            up_ref[at].astype(F32) + inv_std * (input_grad - first - scaled * second)
+        ).astype(BF16)
+        return carry
+
+    lax.fori_loop(0, pair_ref.shape[0], back, 0)
+    shape = parts_ref.shape[:2]
+    parts_ref[:, :, :wide] = total_ref[...].reshape(shape + (wide,))
+    parts_ref[:, :, wide:] = rest_ref[...].reshape(shape + (rest_ref.shape[1],))
+
+    def copy(step, src, dst, at):
+        to_row, to_col = partner(step, rows, chan)
+        return pltpu.make_async_remote_copy(
+            src,
+            dst,
+            small_send.at[at, step],
+            small_recv.at[at, step],
+            device_id=(to_row, to_col),
+            device_id_type=MESH,
+        )
+
+    def spread(step):
+        return copy(step, parts_ref.at[partner(step, rows, chan)[1]], from_chan.at[col], 0)
+
+    def across(step):
+        return copy(step * chan, held_ref, from_rows.at[row], 1)
+
+    def share(step):
+        return copy(step, mine_ref, sums_ref.at[col], 2)
+
+    def run(make, count):
+        lax.fori_loop(1, count, lambda step, carry: (make(step).start(), carry)[1], 0)
+        lax.fori_loop(1, count, lambda step, carry: (make(step).wait(), carry)[1], 0)
+
+    from_chan[col] = parts_ref[col]
+    run(spread, chan)
+    held_ref[...] = jnp.sum(from_chan[...], axis=0)
+    from_rows[row] = held_ref[...]
+    run(across, rows)
+    mine_ref[...] = jnp.sum(from_rows[...], axis=0) * (1.0 / tokens)
+    sums_ref[col] = mine_ref[...]
+    run(share, chan)
+    wait_all(rows, chan, tri_in, tri_ref, send, recv, 0)
+
+
+def finish_back(rows, chan, tri_two, by_pair, weights, rest):
+    vmem = pl.BlockSpec(memory_space=pltpu.VMEM)
+    channels, wide = weights[1].shape
+    part, width = channels // chan, wide + rest.shape[1]
+    operands = [tri_two, *by_pair, *weights, rest]
+    held = [(channels, wide), (chan, part, width), (chan, part, width), (part, width)]
+    held += [(rows, part, width), (part, width)]
+    count = rows * chan
+    return pl.pallas_call(
+        functools.partial(tail_kernel, rows, chan),
+        in_specs=[vmem] * len(operands),
+        out_specs=[vmem] * 3,
+        out_shape=[
+            jax.ShapeDtypeStruct(tri_two.shape, BF16),
+            jax.ShapeDtypeStruct(by_pair[0].shape, BF16),
+            jax.ShapeDtypeStruct((chan, part, width), F32),
+        ],
+        scratch_shapes=[pltpu.VMEM(h, F32) for h in held]
+        + [pltpu.SemaphoreType.DMA((1, count))] * 2
+        + [pltpu.SemaphoreType.DMA((3, count))] * 2,
+        compiler_params=pltpu.CompilerParams(
+            collective_id=3, has_side_effects=True, vmem_limit_bytes=GRANT
+        ),
+        name="finish_back",
+    )(*operands)
 
 
 def few_shards(
@@ -315,7 +382,6 @@
     long, short, channels = pair_rep.shape
     hidden = out_final.shape[0]
     per = hidden // (rows * chan)
-    tokens = long * rows
 
     def to_slab(values):
         return jnp.swapaxes(values, 0, 1).reshape(rows * chan, per, short, long)
@@ -345,19 +411,15 @@
     left_grad, right_grad, tri_two = fused(
         backward_kernel, rows, chan, slabs, 3, 5, 5, 2, "backward"
     )
-    tri_two = exchange(tri_two)
-    grad_pair, grad_proj = pairwise(
-        back_kernel,
+    tri_two, grad_pair, grads = finish_back(
+        rows,
+        chan,
+        tri_two,
         [pair, up, pre_grad, to_pairs(left_grad), to_pairs(right_grad)],
         [out_proj_t, out_proj, out_gate],
-        1,
-        [out_proj.shape],
-        "back",
-    )
-    grads = jnp.concatenate([grad_proj, grad_gate, grad_final], 1)
-    grads = jnp.sum(exchange(grads).reshape(rows * chan, per, -1), 0) / tokens
-    grads = exchange(jnp.broadcast_to(grads[None], (rows * chan,) + grads.shape))
-    grads = grads.reshape(hidden, -1)
+        jnp.concatenate([grad_gate, grad_final], 1),
+    )
+    grads = grads.reshape(channels, -1)
     (final_pair,) = pairwise(
         final_kernel,
         [to_pairs(tri_two), middle, column(in_drop)],
@@ -528,7 +590,7 @@
 def solution(mesh):
     rows, chan = mesh.shape["rows"], mesh.shape["chan"]
     few = H % (rows * chan) == 0 and chan % rows == 0 and rows & (rows - 1) == 0 and chan & (chan - 1) == 0
-    few = few and N // rows >= 128 and N // chan >= 16
+    few = few and H % (8 * chan) == 0 and N // rows >= 128 and N // chan >= 16
     shard = functools.partial(few_shards, rows, chan) if few else shards
     in_specs = (
         P("rows", "chan", None),

time: 560 us -> 544 us (0.971)
  Pallas kernels: 438 us -> 503 us
  waiting for transfers between devices: 44.5 us -> 0 us
  blocking collectives: 34.7 us -> 0 us
    pallas_call x0 -> x1, Pallas kernels: none -> 79.4 us  [finish_back(): pl.pallas_call(functools.partial(tail_kernel, rows, chan), in_specs=[vmem...]
    all_to_all x1 -> x0, waiting for transfers between devices: 44.5 us -> none  [exchange(): return lax.all_to_all(values, BOTH, split_axis=0, concat_axis=0, tiled=True)]
    all_to_all x2 -> x0, blocking collectives: 34.7 us -> none  [exchange(): return lax.all_to_all(values, BOTH, split_axis=0, concat_axis=0, tiled=True)]
    pallas_call x4 -> x3, Pallas kernels: 35.5 us -> 22.7 us  [pairwise(): pl.pallas_call(kernel, grid=(steps,), in_specs=[cut(a) for a in by_pair]...]
    unnamed x42 -> x48, local copies, waits for them, and re-layouts: 21 us -> 21.3 us
  transfers between devices with their start and end apart: 1 -> 0, of which waited for: 1 -> 0; matrix products, arithmetic and copies ran while one was open for 1% -> 0% of each run, Pallas kernels for 0% -> 0%
where the time goes in v3:
time: 544 us
  Pallas kernels  503 us (92%)
  local copies, waits for them, and re-layouts  39.3 us (7%)
    pallas_call x2, Pallas kernels, fused(): pl.pallas_call(functools.partial(kernel, rows, chan), in_specs=[vmem] * l...  401 us
    pallas_call x1, Pallas kernels, finish_back(): pl.pallas_call(functools.partial(tail_kernel, rows, chan), in_specs=[vmem...  79.4 us
    pallas_call x3, Pallas kernels, pairwise(): pl.pallas_call(kernel, grid=(steps,), in_specs=[cut(a) for a in by_pair]...  22.7 us
    unnamed x48, local copies, waits for them, and re-layouts  21.3 us

profile of v3, /device:TPU:0, one launch (start us, length us, event | category | flops | bytes accessed | tf_op | source)
XLA Modules:
  0.0 543.6 jit_solution(17582811694423310606)
XLA Ops:
  0.6 3.0 copy.55
  3.7 0.1 copy.56
  3.8 4.2 front.1
  8.0 1.2 copy.57
  9.2 1.2 copy.58
  10.4 158.9 %outgoing.1 = (bf16[32,4,32,256]{3,2,1,0:T(8,128)(2,1)S(1)}, bf16[32,4,32,256]{3,2,1,0:T(8,128)(2,1)S(1)}, bf16[32,4,32,256]{3,2,1,0:T(8,128)(2,1)S(1)}) custom-call(bf16[32,4,32,256]{3,2,1,0:T(8,128)(2,1)S(1)} %bitcast.47, bf16[32,4,32,256]{3,2,1,0:T(8,128)(2,1)S(1)} %bitcast.48), custom_call_target="tpu_custom_call" | custom-call | tf_op jit(solution)/shard_map/outgoing/pallas_call | solution.py:257
  169.3 1.2 copy.85
  170.6 0.7 copy-done.6
  171.3 4.3 copy.60
  175.6 2.0 copy.64.drop_ref
  177.6 0.1 copy.63
  177.7 0.1 copy.61
  177.9 0.1 copy.62
  178.0 14.6 %middle.1 = (bf16[32,128,256]{2,1,0:T(8,128)(2,1)S(1)}, bf16[32,128,256]{2,1,0:T(8,128)(2,1)S(1)}, bf16[32,128,256]{2,1,0:T(8,128)(2,1)S(1)}, bf16[32,128,256]{2...) custom-call(bf16[32,128,256]{2,1,0:T(8,128)(2,1)S(1)} %bitcast.49, ...), custom_call_target="tpu_custom_call" | custom-call | tf_op jit(solution)/shard_map/middle/pallas_call | solution.py:100
  192.6 1.2 copy.65
  193.8 0.1 copy-done.9
  193.9 1.2 copy.66
  195.1 1.2 copy.67
  196.3 242.3 %backward.1 = (bf16[32,4,32,256]{3,2,1,0:T(8,128)(2,1)S(1)}, bf16[32,4,32,256]{3,2,1,0:T(8,128)(2,1)S(1)}, bf16[32,4,32,256]{3,2,1,0:T(8,128)(2,1)S(1)}) custom-call(bf16[32,4,32,256]{3,2,1,0:T(8,128)(2,1)S(1)} %bitcast.44, bf16[32,4,32,256]{3,2,1,0:T(8,128)(2,1)S(1)} %bitcast.45, bf16[32,4,32,256]{3,2,1,0:T(8,128)(2,1)S(1)} %bitcast.46, ...), custom_call_target="tpu_custom_call" | custom-call | tf_op jit(solution)/shard_map/backward/pallas_call | solution.py:257
  438.6 4.4 copy_bitcast_fusion.1
  443.1 79.4 %finish_back.1 = (bf16[32,4,32,256]{3,2,1,0:T(8,128)(2,1)S(1)}, bf16[32,128,256]{2,1,0:T(8,128)(2,1)S(1)}, f32[16,8,768]{2,1,0:T(8,128)S(1)}) custom-call(bf16[32,4,32,256]{3,2,1,0:T(8,128)(2,1)S(1)} %get-tuple-element.31.tri_in, bf16[32,128,256]{2,1,0:T(8,128)(2,1)S(1)} %bitcast.41, bf16[32,128,256]{2,1,0:T(8,128)(2,1)S(1)} %bitcast.43, ...), custom_call_target="tpu_custom_call" | custom-call | tf_op jit(solution)/shard_map/finish_back/pallas_call | solution.py:359
  522.5 1.2 copy.84
  523.8 2.0 copy.73.drop_ref
  525.9 0.1 copy.72
  526.1 1.6 copy-done.3
  527.6 1.6 copy-done.10
  529.2 3.9 final.1
  533.2 1.3 copy-done.4
  534.5 4.6 copy.74
  539.1 3.0 copy.75
  542.2 0.7 slice.12
  542.9 0.7 fusion
  (37 shorter events, 0.4 us)
Async XLA Ops:
  0.6 3.1 copy-start.11
  3.7 5.5 %copy-start = (bf16[256,32,128]{0,2,1:T(8,128)(2,1)}, bf16[256,32,128]{0,2,1:T(8,128)(2,1)S(1)}, u32[]{:S(2)}) copy-start(bf16[256,32,128]{0,2,1:T(8,128)(2,1)S(1)} %copy.55) | copy-start | bytes 6291460
  169.3 1.3 copy-start.5
  169.3 2.0 copy-start.6
  171.3 4.3 copy-start.17
  175.6 2.0 copy-start.14
  175.6 2.1 copy-start.13
  175.6 2.3 copy-start.12
  192.6 1.3 copy-start.9
  438.6 4.4 copy-start.1
  438.6 4.4 copy-start.2
  522.5 1.3 copy-start.7
  522.5 1.3 copy-start.18
  523.8 2.0 copy-start.15
  523.8 2.1 copy-start.16
  526.0 1.6 copy-start.3
  527.6 1.6 copy-start.10
  533.2 1.3 copy-start.4
  534.5 4.6 copy-start.8
